TPU v7x, 256 devices: a whole 4x4x8 slice. The times are simulated.
256 devices in a mesh: blk: 64 (over y, x_lo, z), rep: 4 (over x_hi, core).
Axes of the slice: x: 4 (x_hi: 2, x_lo: 2; x = x_hi * 2 + x_lo), y: 4, z: 8, core: 2. Of those that a mesh axis runs over, the one named last changes fastest.
Arguments:
- image_feats: bfloat16 [131072, 1152], P(('blk', 'rep')), may hold values from -16 to 16, as said below
- text_feats: bfloat16 [131072, 1152], P(('blk', 'rep')), may hold values from -16 to 16, as said below
- head: bfloat16 [1152, 1152], replicated, may hold values from -0.1875 to 0.1875
- image_ids: int32 [131072], P(('blk', 'rep')), may hold values from 0 to 2047
- text_ids: int32 [131072], P(('blk', 'rep')), may hold values from 0 to 2047
- log_scale: float32 [1], replicated, may hold values from 3 to 3.7
- bias: float32 [1], replicated, may hold values from -3 to -1
Outputs:
- grad_image_feats: bfloat16 [131072, 1152], P(('blk', 'rep'))
- grad_text_feats: bfloat16 [131072, 1152], P(('blk', 'rep'))
- grad_head: float32 [1152, 1152], P('blk')
Inputs may be any that keep to these rules, and one draw needn't show every extreme that they name: `image_feats`: row magnitudes differ from row to row. `text_feats`: row magnitudes differ from row to row.
All inputs are finite; a program needn't handle non-finite values.
Results may differ from a plain program's by a relative error of at most 0.0072.
Values may be sent and summed in bfloat16 or wider, within the bound.
No kernel may reach another device: no remote copies, remote signals or barrier semaphores. Data moves between devices by JAX's collectives and lax.ppermute only.
A program may use at most 128 MiB of HBM per device.

v0:
```python
import jax
import jax.numpy as jnp
from jax import lax
from jax.sharding import PartitionSpec as P

HOPS = 4


def shifted(value, axis, steps):
    count = lax.axis_size(axis)
    pairs = [(source, (source + steps) % count) for source in range(count)]
    return lax.ppermute(value, axis, pairs)


def unit_rows(values):
    inverse = lax.rsqrt(jnp.sum(values * values, axis=-1, keepdims=True) + 1e-06)
    return (values * inverse, inverse)


def per_device(image_feats, text_feats, head, image_ids, text_ids, log_scale, bias):
    u_local = jnp.dot(image_feats, head, preferred_element_type=jnp.float32)
    x_full, inv_u = unit_rows(u_local)
    x_half = x_full.astype(jnp.bfloat16)
    y_full, inv_t = unit_rows(text_feats.astype(jnp.float32))
    y_half = y_full.astype(jnp.bfloat16)
    scale = jnp.exp(log_scale[0])
    offset = bias[0]

    def coefficients(images, image_labels, texts, text_labels):
        logits = (
            scale * jnp.einsum("id,jd->ij", images, texts, preferred_element_type=jnp.float32)
            + offset
        )
        positive = (image_labels[:, None] == text_labels[None, :]).astype(jnp.float32)
        return (scale * (jax.nn.sigmoid(logits) - positive)).astype(jnp.bfloat16)

    def tile(block, block_ids):
        coef = coefficients(x_half, image_ids, block, block_ids)
        image_part = jnp.dot(coef, block, preferred_element_type=jnp.float32)
        text_part = jnp.einsum("ij,id->jd", coef, x_half, preferred_element_type=jnp.float32)
        return (image_part, text_part)

    grad_x, text_sum = tile(y_half, text_ids)
    block, block_ids = (y_half, text_ids)
    for hop in range(1, HOPS + 1):
        block = shifted(block, "blk", 1)
        block_ids = shifted(block_ids, "blk", 1)
        image_part, text_part = tile(block, block_ids)
        grad_x = grad_x + image_part
        text_sum = shifted(text_sum, "blk", 1) + text_part
    grad_y = shifted(text_sum, "blk", -HOPS)
    grad_u = (inv_u * (grad_x - x_full * jnp.sum(x_full * grad_x, axis=1, keepdims=True))).astype(
        jnp.bfloat16
    )
    grad_image = jnp.einsum("id,ed->ie", grad_u, head, preferred_element_type=jnp.float32).astype(
        jnp.bfloat16
    )
    cycle_rows = lax.psum_scatter(
        jnp.einsum("ie,id->ed", image_feats, grad_u, preferred_element_type=jnp.float32),
        "blk",
        scatter_dimension=0,
        tiled=True,
    )
    devices_all = lax.axis_size("blk") * lax.axis_size("rep")
    grad_head = lax.psum(cycle_rows, "rep") / devices_all
    grad_text = (
        inv_t * (grad_y - y_full * jnp.sum(y_full * grad_y, axis=1, keepdims=True))
    ).astype(jnp.bfloat16)
    return (grad_image, grad_text, grad_head)


def solution(mesh):
    placed = (
        P(("blk", "rep"), None),
        P(("blk", "rep"), None),
        P(),
        P(("blk", "rep")),
        P(("blk", "rep")),
        P(),
        P(),
    )
    return jax.shard_map(
        per_device,
        mesh=mesh,
        in_specs=placed,
        out_specs=(P(("blk", "rep"), None), P(("blk", "rep"), None), P("blk", None)),
        check_vma=False,
    )
```

profile of v0, /device:TPU:1, one launch (start us, length us, event | category | flops | bytes accessed | tf_op | source)
XLA Modules:
  0.0 1003.0 jit_solution(10093257569630580109)
XLA Ops:
  7.2 1.7 fusion.7
  9.0 0.3 fusion.2
  9.3 2.5 collective-permute-start
  11.8 2.0 multiply_reduce_fusion.1
  15.2 0.2 multiply_convert_fusion.1
  15.4 0.4 copy-done.9
  15.8 1.1 fusion.43
  16.9 0.9 fusion.49
  17.8 1.7 collective-permute-start.8
  19.5 25.3 %collective-permute-done = bf16[512,1152]{1,0:T(8,128)(2,1)S(1)} collective-permute-done((bf16[512,1152]{1,0:T(8,128)(2,1)S(1)}, bf16[512,1152]{1,0:T(8,128)(2,1)S(1)}, u32[]{:S(2)}, u32[]{:S(2)}) %collective-permute-start) | collective-permute-done | bytes 1179680 | tf_op jit(solution)/shard_map/ppermute | solution.py:12
  44.8 75.9 %collective-permute-done.1 = s32[512]{0:T(512)S(1)} collective-permute-done((s32[512]{0:T(512)S(1)}, s32[512]{0:T(512)S(1)}, u32[]{:S(2)}, u32[]{:S(2)}) %collective-permute-start.1) | collective-permute-done | bytes 2080 | tf_op jit(solution)/shard_map/ppermute | solution.py:12
  120.7 6.7 collective-permute-done.3
  127.4 1.1 fusion.44
  128.6 0.9 convolution_add_fusion
  129.5 0.3 collective-permute-start.9
  129.7 0.8 fusion.48
  130.6 3.4 collective-permute-done.5
  134.0 0.9 convolution_add_fusion.4
  134.9 1.1 fusion.45
  136.0 21.9 %collective-permute-done.4 = bf16[512,1152]{1,0:T(8,128)(2,1)S(1)} collective-permute-done((bf16[512,1152]{1,0:T(8,128)(2,1)S(1)}, bf16[512,1152]{1,0:T(8,128)(2,1)S(1)}, u32[]{:S(2)}, u32[]{:S(2)}) %collective-permute-start.4) | collective-permute-done | bytes 1179680 | tf_op jit(solution)/shard_map/ppermute | solution.py:12
  157.9 0.9 fusion.50
  158.8 0.9 convolution_add_fusion.3
  159.6 1.1 fusion.46
  160.7 0.9 convolution_add_fusion.2
  161.6 46.8 %collective-permute-done.9 = f32[512,1152]{1,0:T(8,128)S(1)} collective-permute-done((f32[512,1152]{1,0:T(8,128)S(1)}, f32[512,1152]{1,0:T(8,128)S(1)}, u32[]{:S(2)}, u32[]{:S(2)}) %collective-permute-start.9) | collective-permute-done | bytes 2359328 | tf_op jit(solution)/shard_map/ppermute | solution.py:12
  208.5 1.7 add.99
  210.2 23.6 %collective-permute-done.6 = bf16[512,1152]{1,0:T(8,128)(2,1)S(1)} collective-permute-done((bf16[512,1152]{1,0:T(8,128)(2,1)S(1)}, bf16[512,1152]{1,0:T(8,128)(2,1)S(1)}, u32[]{:S(2)}, u32[]{:S(2)}) %collective-permute-start.6) | collective-permute-done | bytes 1179680 | tf_op jit(solution)/shard_map/ppermute | solution.py:12
  233.8 1.1 fusion.47
  234.9 1.1 multiply_reduce_fusion
  236.0 0.4 multiply_convert_fusion
  236.4 1.0 copy-done.5
  237.4 4.1 convolution_bitcast_fusion
  241.6 2.1 fusion.51
  243.8 47.0 %collective-permute-done.10 = f32[512,1152]{1,0:T(8,128)} collective-permute-done((f32[512,1152]{1,0:T(8,128)}, f32[512,1152]{1,0:T(8,128)}, u32[]{:S(2)}, u32[]{:S(2)}) %collective-permute-start.10) | collective-permute-done | bytes 2359328 | tf_op jit(solution)/shard_map/ppermute | solution.py:12
  290.8 2.0 add.100
  292.8 0.3 collective-permute-start.11
  293.1 0.9 fusion.52
  294.0 65.8 %collective-permute-done.11 = f32[512,1152]{1,0:T(8,128)S(1)} collective-permute-done((f32[512,1152]{1,0:T(8,128)S(1)}, f32[512,1152]{1,0:T(8,128)S(1)}, u32[]{:S(2)}, u32[]{:S(2)}) %collective-permute-start.11) | collective-permute-done | bytes 2359328 | tf_op jit(solution)/shard_map/ppermute | solution.py:12
  359.8 1.7 add.101
  361.5 0.6 dynamic-slice
  362.8 539.7 %all-reduce.6.cloned.1.call-done = f32[1152,1152]{0,1:T(8,128)} async-done(((f32[1152,1152]{0,1:T(8,128)}), f32[1152,1152]{0,1:T(8,128)}) %all-reduce.6.cloned.1.call-update) | async-done | bytes 5308432
  902.5 2.3 constant_dynamic-slice_fusion
  904.8 4.1 convolution_convert_fusion
  909.0 79.4 %all-reduce.4.cloned.1.call-done = f32[18,1152]{0,1:T(8,128)} async-done(((f32[18,1152]{0,1:T(8,128)}), f32[18,1152]{0,1:T(8,128)}) %all-reduce.4.cloned.1.call-update) | async-done | bytes 82960 | tf_op jit(solution)/shard_map/psum | solution.py:65
  988.4 1.1 broadcast_multiply_fusion
  989.6 0.9 copy.11
  990.4 2.5 fusion.3
  993.0 3.2 fusion.6
  (41 shorter events, 0.3 us)
Async XLA Ops:
  7.2 4.7 copy-start
  7.2 895.3 %all-reduce.6.cloned.1.call-start = ((), (), s32[]{:S(2)}) async-start(), calls=%async_computation.1 | async-start | bytes 10616832
  7.2 1.8 copy-start.3
  9.0 2.8 copy-start.8
  9.3 35.6 %collective-permute-start = (bf16[512,1152]{1,0:T(8,128)(2,1)S(1)}, bf16[512,1152]{1,0:T(8,128)(2,1)S(1)}, u32[]{:S(2)}, u32[]{:S(2)}) collective-permute-start(bf16[512,1152]{1,0:T(8,128)(2,1)S(1)} %fusion.2), channel_id=1, source_target_pairs={{0,4},{4,8},{8,12},{12,16},{16,20},{20,24},{24,28},{28,32},{32,36}... | collective-permute-start | bytes 3538952 | tf_op jit(solution)/shard_map/ppermute | solution.py:12
  15.1 0.7 copy-start.9
  15.2 0.7 copy-start.10
  15.4 218.4 %copy-start.1 = (bf16[512,1152]{1,0:T(8,128)(2,1)}, bf16[512,1152]{1,0:T(8,128)(2,1)S(1)}, u32[]{:S(2)}) copy-start(bf16[512,1152]{1,0:T(8,128)(2,1)S(1)} %multiply_convert_fusion.1) | copy-start | bytes 3538948
  17.8 110.7 %collective-permute-start.8 = (f32[512,1152]{1,0:T(8,128)S(1)}, f32[512,1152]{1,0:T(8,128)S(1)}, u32[]{:S(2)}, u32[]{:S(2)}) collective-permute-start(f32[512,1152]{1,0:T(8,128)S(1)} %fusion.49), channel_id=1, source_target_pairs={{0,4},{4,8},{8,12},{12,16},{16,20},{20,24},{24,28},{28,32},{32,36}... | collective-permute-start | bytes 7077896 | tf_op jit(solution)/shard_map/ppermute | solution.py:12
  44.8 83.6 %collective-permute-start.2 = (bf16[512,1152]{1,0:T(8,128)(2,1)S(1)}, bf16[512,1152]{1,0:T(8,128)(2,1)S(1)}, u32[]{:S(2)}, u32[]{:S(2)}) collective-permute-start(bf16[512,1152]{1,0:T(8,128)(2,1)S(1)} %collective-permute-done), channel_id=1, source_target_pairs={{0,4},{4,8},{8,12},{12,16},{16,20},{20,24},{24,28},{28,32},{32,36}... | collective-permute-start | bytes 3538952 | tf_op jit(solution)/shard_map/ppermute | solution.py:12
  44.8 75.9 %collective-permute-start.1 = (s32[512]{0:T(512)S(1)}, s32[512]{0:T(512)S(1)}, u32[]{:S(2)}, u32[]{:S(2)}) collective-permute-start(s32[512]{0:T(512)S(1)} %copy-done.9), channel_id=1, source_target_pairs={{0,4},{4,8},{8,12},{12,16},{16,20},{20,24},{24,28},{28,32},{32,36}... | collective-permute-start | bytes 6152 | tf_op jit(solution)/shard_map/ppermute | solution.py:12
  120.7 6.7 collective-permute-start.3
  127.4 6.7 collective-permute-start.5
  128.5 29.4 %collective-permute-start.4 = (bf16[512,1152]{1,0:T(8,128)(2,1)S(1)}, bf16[512,1152]{1,0:T(8,128)(2,1)S(1)}, u32[]{:S(2)}, u32[]{:S(2)}) collective-permute-start(bf16[512,1152]{1,0:T(8,128)(2,1)S(1)} %collective-permute-done.2), channel_id=1, source_target_pairs={{0,4},{4,8},{8,12},{12,16},{16,20},{20,24},{24,28},{28,32},{32,36}... | collective-permute-start | bytes 3538952 | tf_op jit(solution)/shard_map/ppermute | solution.py:12
  129.5 79.0 %collective-permute-start.9 = (f32[512,1152]{1,0:T(8,128)S(1)}, f32[512,1152]{1,0:T(8,128)S(1)}, u32[]{:S(2)}, u32[]{:S(2)}) collective-permute-start(f32[512,1152]{1,0:T(8,128)S(1)} %convolution_add_fusion), channel_id=1, source_target_pairs={{0,4},{4,8},{8,12},{12,16},{16,20},{20,24},{24,28},{28,32},{32,36}... | collective-permute-start | bytes 7077896 | tf_op jit(solution)/shard_map/ppermute | solution.py:12
  134.0 76.1 %collective-permute-start.7 = (s32[512]{0:T(512)S(1)}, s32[512]{0:T(512)S(1)}, u32[]{:S(2)}, u32[]{:S(2)}) collective-permute-start(s32[512]{0:T(512)S(1)} %collective-permute-done.5), channel_id=1, source_target_pairs={{0,4},{4,8},{8,12},{12,16},{16,20},{20,24},{24,28},{28,32},{32,36}... | collective-permute-start | bytes 6152 | tf_op jit(solution)/shard_map/ppermute | solution.py:12
  157.9 75.9 %collective-permute-start.6 = (bf16[512,1152]{1,0:T(8,128)(2,1)S(1)}, bf16[512,1152]{1,0:T(8,128)(2,1)S(1)}, u32[]{:S(2)}, u32[]{:S(2)}) collective-permute-start(bf16[512,1152]{1,0:T(8,128)(2,1)S(1)} %collective-permute-done.4), channel_id=1, source_target_pairs={{0,4},{4,8},{8,12},{12,16},{16,20},{20,24},{24,28},{28,32},{32,36}... | collective-permute-start | bytes 3538952 | tf_op jit(solution)/shard_map/ppermute | solution.py:12
  210.2 80.6 %collective-permute-start.10 = (f32[512,1152]{1,0:T(8,128)}, f32[512,1152]{1,0:T(8,128)}, u32[]{:S(2)}, u32[]{:S(2)}) collective-permute-start(f32[512,1152]{1,0:T(8,128)} %add.99), channel_id=1, source_target_pairs={{0,4},{4,8},{8,12},{12,16},{16,20},{20,24},{24,28},{28,32},{32,36}... | collective-permute-start | bytes 7077896 | tf_op jit(solution)/shard_map/ppermute | solution.py:12
  234.9 1.1 copy-start.6
  236.4 1.0 copy-start.5
  241.6 746.9 %all-reduce.4.cloned.1.call-start = ((), (), s32[]{:S(2)}) async-start(), calls=%async_computation | async-start | bytes 1179648 | tf_op jit(solution)/shard_map/psum | solution.py:65
  243.8 49.3 %copy-start.2 = (bf16[512,1152]{1,0:T(8,128)(2,1)S(1)}, bf16[512,1152]{1,0:T(8,128)(2,1)}, u32[]{:S(2)}) copy-start(bf16[512,1152]{1,0:T(8,128)(2,1)} %copy-done.1) | copy-start | bytes 3538948
  243.8 49.3 %copy-start.7 = (bf16[512,512]{1,0:T(8,128)(2,1)S(1)}, bf16[512,512]{1,0:T(8,128)(2,1)}, u32[]{:S(2)}) copy-start(bf16[512,512]{1,0:T(8,128)(2,1)} %copy-done.6) | copy-start | bytes 1572868
  292.8 67.1 %collective-permute-start.11 = (f32[512,1152]{1,0:T(8,128)S(1)}, f32[512,1152]{1,0:T(8,128)S(1)}, u32[]{:S(2)}, u32[]{:S(2)}) collective-permute-start(f32[512,1152]{1,0:T(8,128)S(1)} %add.100), channel_id=1, source_target_pairs={{0,4},{4,8},{8,12},{12,16},{16,20},{20,24},{24,28},{28,32},{32,36}... | collective-permute-start | bytes 7077896 | tf_op jit(solution)/shard_map/ppermute | solution.py:12
  294.0 67.6 %copy-start.11 = (u32[256]{0:T(256)S(1)}, u32[256]{0:T(256)}, u32[]{:S(2)}) copy-start(u32[256]{0:T(256)} %constant.11) | copy-start | bytes 3076
  361.5 628.9 %collective-permute-start.12 = (f32[512,1152]{1,0:T(8,128)}, f32[512,1152]{1,0:T(8,128)}, u32[]{:S(2)}, u32[]{:S(2)}) collective-permute-start(f32[512,1152]{1,0:T(8,128)} %add.101), channel_id=1, source_target_pairs={{0,240},{4,244},{8,248},{12,252},{16,0},{20,4},{24,8},{28,12},{32,... | collective-permute-start | bytes 7077896 | tf_op jit(solution)/shard_map/ppermute | solution.py:12
  990.4 2.5 copy-start.4
Sparse Core Ops, SparseCore 0:
  241.7 660.7 all-reduce.5
  905.1 83.2 all-reduce.3
where the time goes:
time: 1000 us
  waiting for transfers between devices  936 us (94%)
  matrix products  25.8 us (3%)
  between operations  16.3 us (2%)
  other arithmetic  14.8 us (1%)
    unnamed x3, waiting for transfers between devices  540 us
    ppermute x13, waiting for transfers between devices, shifted(): return lax.ppermute(value, axis, pairs)  316 us
    psum x1, waiting for transfers between devices, per_device(): grad_head = lax.psum(cycle_rows, 'rep') / devices_all  79.4 us
  transfers between devices with their start and end apart: 15, of which 11 were waited for; matrix products, arithmetic and copies ran while one was open for 4% of the time, Pallas kernels for 0%

commit v1 on v0

v1 whole, which is shorter than its diff:
```python
import jax
import jax.numpy as jnp
from jax import lax
from jax.experimental import pallas as pl
from jax.experimental.pallas import tpu as pltpu
from jax.sharding import Mesh, PartitionSpec as P

AXES = ("y", "xl", "z", "xh", "c")
CYCLE = ("y", "xl", "z")
F32 = jnp.float32
BF16 = jnp.bfloat16
D = 1152
ROWS = 512
SENT = 528
STEP = 256
WIDE = 640
PART = 384


def shifted(value, steps):
    count = lax.axis_size(CYCLE)
    return lax.ppermute(value, CYCLE, [(i, (i + steps) % count) for i in range(count)])


def after(value, *others):
    return lax.optimization_barrier((value,) + others)[0]


def nn(a, b):
    return jnp.dot(a, b, preferred_element_type=F32)


def nt(a, b):
    return lax.dot_general(a, b, (((1,), (1,)), ((), ())), preferred_element_type=F32)


def run(kernel, outs, *args, scalars=1, aliases=None, vmem=40):
    specs = [pl.BlockSpec(memory_space=pltpu.SMEM)] * scalars
    specs += [pl.BlockSpec(memory_space=pltpu.VMEM)] * (len(args) - scalars)
    return pl.pallas_call(
        kernel,
        out_shape=[jax.ShapeDtypeStruct(s, t) for s, t in outs],
        in_specs=specs,
        out_specs=[pl.BlockSpec(memory_space=pltpu.VMEM)] * len(outs),
        input_output_aliases=aliases or {},
        compiler_params=pltpu.CompilerParams(vmem_limit_bytes=vmem * 2**20),
        cost_estimate=pl.CostEstimate(flops=0, bytes_accessed=0, transcendentals=0),
    )(*args)


def steps(body):
    @pl.loop(0, ROWS // STEP)
    def _(i):
        body(pl.ds(pl.multiple_of(i * STEP, STEP), STEP))


def inverse_norm(values):
    return lax.rsqrt(jnp.sum(values * values, axis=-1, keepdims=True) + 1e-06)


def lane_ids(block):
    pair = block[pl.ds(ROWS, 16), pl.ds(0, ROWS)].astype(F32)
    return pair[0:1] * 256.0 + pair[1:2]


def coef_of(par, rows, row_ids, columns, column_ids):
    scale, offset = par[0], par[1]
    logits = scale * nt(rows, columns) + offset
    positive = (row_ids == column_ids).astype(F32)
    return (scale * (jax.nn.sigmoid(logits) - positive)).astype(BF16)


def unit_images(feats, head, full, inverse, half, feats_t):
    def body(r):
        u = nn(feats[r, :], head[...])
        inv = inverse_norm(u)
        x = u * inv
        half[r, :] = x.astype(BF16)
        if full is not None:
            full[r, :] = x
            inverse[r, :] = inv

    steps(body)
    if feats_t is not None:

        @pl.loop(0, D // 128)
        def _(k):
            cols = pl.ds(pl.multiple_of(k * 128, 128), 128)
            feats_t[cols, :] = feats[pl.ds(0, ROWS), cols].T


def project(inv, grad, x):
    return inv * (grad - x * jnp.sum(x * grad, axis=1, keepdims=True))


def prepare(text, image, text_lane, image_lane, text_out, image_out):
    def body(r):
        t = text[r, :].astype(F32)
        text_out[r, :] = (t * inverse_norm(t)).astype(BF16)
        image_out[r, :] = image[r, :]

    steps(body)
    for lane, out in ((text_lane, text_out), (image_lane, image_out)):
        out[pl.ds(ROWS, 16), :] = jnp.zeros((16, D), BF16)
        row = lax.broadcasted_iota(jnp.int32, (16, ROWS), 0)
        ids = lane[...]
        high, low = (ids >> 8).astype(F32), (ids & 255).astype(F32)
        pair = jnp.where(row == 0, high, jnp.where(row == 1, low, 0.0))
        out[pl.ds(ROWS, 16), pl.ds(0, ROWS)] = pair.astype(BF16)


def first(par, head, a0, y0, iid, tid, full, inv, half, a_t, gx, gy):
    unit_images(a0, head, full, inv, half, a_t)
    t_lane, i_lane = lane_ids(y0), lane_ids(a0)
    text = y0[pl.ds(0, ROWS), :]

    def body(r):
        gx[r, :] = nn(coef_of(par, half[r, :], iid[r, :], text, t_lane), text)
        gy[r, :] = nn(coef_of(par, y0[r, :], tid[r, :], half[...], i_lane), half[...])

    steps(body)


def second(par, head, a1, y1, x0, y0, iid, tid, gx0, gy0, full, inv, half, a_t, gx, gy):
    unit_images(a1, head, full, inv, half, a_t)
    t_lane, i_lane = lane_ids(y1), lane_ids(a1)
    text = y1[pl.ds(0, ROWS), :]

    def body(r):
        gx[r, :] = gx0[r, :] + nn(coef_of(par, x0[r, :], iid[r, :], text, t_lane), text)
        gy[r, :] = gy0[r, :] + nn(
            coef_of(par, y0[r, :], tid[r, :], half[...], i_lane), half[...]
        )

    steps(body)


def third(par, head, a2, y2, x0, f0, v0, x1, f1, v1, iid, ids1, ids2, gx0,
          half, a_t, u0, u1, u2, gx, full, inv):
    unit_images(a2, head, full, inv, half, a_t)
    t_lane = lane_ids(y2)
    text = y2[pl.ds(0, ROWS), :]

    def body(r):
        grad = gx0[r, :] + nn(coef_of(par, x0[r, :], iid[r, :], text, t_lane), text)
        gx[r, :] = grad
        u0[r, :] = project(v0[r, :], grad, f0[r, :]).astype(BF16)
        grad = nn(coef_of(par, x1[r, :], ids1[r, :], text, t_lane), text)
        u1[r, :] = project(v1[r, :], grad, f1[r, :]).astype(BF16)
        grad = nn(coef_of(par, half[r, :], ids2[r, :], text, t_lane), text)
        u2[r, :] = project(inv[r, :], grad, full[r, :]).astype(BF16)

    steps(body)


def head_part(start, a0, a1, a2, u0, u1, u2, out):
    cols = pl.ds(pl.multiple_of(start[0], 128), WIDE)

    @pl.loop(0, D // 384)
    def _(k):
        r = pl.ds(pl.multiple_of(k * 384, 384), 384)
        total = nn(a0[r, :], u0[:, cols])
        total = total + nn(a1[r, :], u1[:, cols])
        total = total + nn(a2[r, :], u2[:, cols])
        out[r, :] = total.astype(out.dtype)


def text_only(par, y0, a2, x2, tid, gy0, gy):
    i_lane = lane_ids(a2)

    def body(r):
        gy[r, :] = gy0[r, :] + nn(coef_of(par, y0[r, :], tid[r, :], x2[...], i_lane), x2[...])

    steps(body)


def to_pieces(mine, away, out):
    @pl.loop(0, 8)
    def _(k):
        r = pl.ds(pl.multiple_of(k * 144, 144), 144)
        total = (mine[r, :] + away[r, :].astype(F32)).astype(BF16)
        out[2 * k] = total[:, :PART]
        out[2 * k + 1] = total[:, 256 : 256 + PART]


def add_pieces(got, out):
    total = got[0].astype(F32)
    for k in range(1, 16):
        total = total + got[k].astype(F32)
    for k in range(8):
        out[k] = total[18 * k : 18 * k + 18]


def add_last(got, out):
    total = got[0]
    for k in range(1, 8):
        total = total + got[k]
    out[...] = total * (1.0 / 256.0)


def fourth(par, head, a3, y3, x0, y0, iid, tid, gx0, gy0, gx, gy, half):
    unit_images(a3, head, None, None, half, None)
    t_lane, i_lane = lane_ids(y3), lane_ids(a3)
    text = y3[pl.ds(0, ROWS), :]

    def body(r):
        gx[r, :] = gx0[r, :] + nn(coef_of(par, x0[r, :], iid[r, :], text, t_lane), text)
        gy[r, :] = gy0[r, :] + nn(
            coef_of(par, y0[r, :], tid[r, :], half[...], i_lane), half[...]
        )

    steps(body)


def last(par, head, a4, y4, x0, y0, iid, tid, gx0, gy0, f0, v0, text_in, g_image, g_text, half):
    unit_images(a4, head, None, None, half, None)
    t_lane, i_lane = lane_ids(y4), lane_ids(a4)
    text = y4[pl.ds(0, ROWS), :]

    def body(r):
        grad = gx0[r, :] + nn(coef_of(par, x0[r, :], iid[r, :], text, t_lane), text)
        grad_u = project(v0[r, :], grad, f0[r, :]).astype(BF16)
        g_image[r, :] = nt(grad_u, head[...]).astype(BF16)
        grad = gy0[r, :] + nn(coef_of(par, y0[r, :], tid[r, :], half[...], i_lane), half[...])
        t = text_in[r, :].astype(F32)
        inv = inverse_norm(t)
        g_text[r, :] = project(inv, grad, t * inv).astype(BF16)

    steps(body)


BLOCK = ((ROWS, D), BF16)
WIDEBLOCK = ((ROWS, D), F32)
COLUMN = ((ROWS, 1), F32)
TURNED = ((D, ROWS), BF16)


def per_device(image_feats, text_feats, head, image_ids, text_ids, log_scale, bias):
    core = lax.axis_index("c")
    par = jnp.stack([jnp.exp(log_scale[0]), bias[0]])
    iid = image_ids.astype(F32).reshape(ROWS, 1)
    tid = text_ids.astype(F32).reshape(ROWS, 1)
    travel = ((SENT, D), BF16)
    y0, a0 = run(
        prepare, [travel, travel], text_feats, image_feats,
        text_ids.reshape(1, ROWS), image_ids.reshape(1, ROWS), scalars=0,
    )
    y1, a1 = shifted(y0, 1), shifted(a0, -1)
    f0, v0, x0, at0, gx, gy = run(
        first, [WIDEBLOCK, COLUMN, BLOCK, TURNED, WIDEBLOCK, WIDEBLOCK],
        par, head, a0, y0, iid, tid,
    )
    y2, a2 = shifted(after(y1, gx), 1), shifted(after(a1, gx), -1)
    f1, v1, x1, at1, gx, gy = run(
        second, [WIDEBLOCK, COLUMN, BLOCK, TURNED, WIDEBLOCK, WIDEBLOCK],
        par, head, a1, y1, x0, y0, iid, tid, gx, gy,
    )
    y3, a3 = shifted(after(y2, gx), 1), shifted(after(a2, gx), -1)

    def column_ids(block):
        pair = block[ROWS : ROWS + 2, :ROWS].astype(F32)
        return (pair[0] * 256.0 + pair[1]).reshape(ROWS, 1)

    x2, at2, u0, u1, u2, gx, _, _ = run(
        third, [BLOCK, TURNED, BLOCK, BLOCK, BLOCK, WIDEBLOCK, WIDEBLOCK, COLUMN],
        par, head, a2, y2, x0, f0, v0, x1, f1, v1, iid, column_ids(a1), column_ids(a2), gx,
    )
    half = ((D, WIDE), BF16)
    (away,) = run(head_part, [half], (512 * (1 - core)).reshape(1), at0, at1, at2, u0, u1, u2)
    got = lax.ppermute(away, "c", [(0, 1), (1, 0)])
    (mine,) = run(
        head_part, [((D, WIDE), F32)],
        after((512 * core).reshape(1), away), at0, at1, at2, u0, u1, u2,
    )
    (gy,) = run(text_only, [WIDEBLOCK], par, y0, a2, x2, tid, after(gy, mine))
    (pieces,) = run(to_pieces, [((16, 144, PART), BF16)], after(mine, gy), got, scalars=0)
    spread = lax.all_to_all(pieces, ("y", "xl", "xh"), 0, 0)
    gx, gy, _ = run(
        fourth, [WIDEBLOCK, WIDEBLOCK, BLOCK],
        par, head, a3, y3, x0, y0, iid, tid, gx, after(gy, pieces),
    )
    y4, a4 = shifted(after(y3, mine), 1), shifted(after(a3, mine), -1)
    (total,) = run(add_pieces, [((8, 18, PART), F32)], after(spread, gx), scalars=0)
    spread = lax.all_to_all(total, "z", 0, 0)
    (total,) = run(add_last, [((18, PART), F32)], spread, scalars=0)
    parts = lax.all_gather(total, ("xh", "c"))
    grad_head = jnp.concatenate(
        [parts[0], parts[2][:, 128:], parts[1][:, 128:], parts[3][:, 128:]], axis=1
    )
    grad_image, grad_text, _ = run(
        last, [BLOCK, BLOCK, BLOCK],
        par, head, a4, y4, x0, y0, iid, tid, gx, after(gy, total), f0, v0, text_feats,
    )
    return grad_image, grad_text, grad_head


def solution(mesh):
    fine = Mesh(mesh.devices.reshape(4, 2, 8, 2, 2), AXES)
    placed = (P(AXES, None), P(AXES, None), P(), P(AXES), P(AXES), P(), P())
    return jax.shard_map(
        per_device,
        mesh=fine,
        in_specs=placed,
        out_specs=(P(AXES, None), P(AXES, None), P(CYCLE, None)),
        check_vma=False,
    )
```

time: 1000 us -> 250 us (0.25)
  waiting for transfers between devices: 936 us -> 73.2 us
  Pallas kernels: 0 us -> 74.4 us
  local copies, waits for them, and re-layouts: 5.32 us -> 38.5 us
  starting transfers between devices: 5.01 us -> 34.9 us
  matrix products: 25.8 us -> 0 us
  blocking collectives: 0 us -> 23.5 us
  between operations: 16.3 us -> 2.21 us
  other arithmetic: 14.8 us -> 2.18 us
    unnamed x3 -> x0, waiting for transfers between devices: 540 us -> none
    ppermute x13 -> x9, waiting for transfers between devices: 316 us -> 53 us  [the longest x8 53 us: shifted(): lax.ppermute(value, CYCLE, [(i, (i + steps) % count) for i in range(count)])]
    psum x1 -> x0, waiting for transfers between devices: 79.4 us -> none  [per_device(): grad_head = lax.psum(cycle_rows, 'rep') / devices_all]
    pallas_call x0 -> x12, Pallas kernels: none -> 74.4 us  [run(): pl.pallas_call(kernel, out_shape=[jax.ShapeDtypeStruct(s, t) for s, t in...]
    unnamed x27 -> x79, local copies, waits for them, and re-layouts: 5.32 us -> 37.2 us
    dot_general x18 -> x0, matrix products: 25.8 us -> none  [the longest x5 5.63 us: tile(): jnp.einsum('ij,id->jd', coef, x_half, preferred_element_type=jnp.float32)]
    ppermute x13 -> x9, starting transfers between devices: 4.93 us -> 30.5 us  [the longest x8 27.6 us: shifted(): lax.ppermute(value, CYCLE, [(i, (i + steps) % count) for i in range(count)])]
    all_to_all x0 -> x1, waiting for transfers between devices: none -> 20.2 us  [per_device(): spread = lax.all_to_all(pieces, ('y', 'xl', 'xh'), 0, 0)]
  transfers between devices with their start and end apart: 15 -> 10, of which waited for: 11 -> 5; matrix products, arithmetic and copies ran while one was open for 4% -> 1% of each run, Pallas kernels for 0% -> 16%
where the time goes in v1:
time: 250 us; the launch traced here: 249 us
  Pallas kernels  74.4 us (30%)
  waiting for transfers between devices  73.2 us (29%)
  local copies, waits for them, and re-layouts  38.5 us (15%)
  starting transfers between devices  34.9 us (14%)
  blocking collectives  23.5 us (9%)
    pallas_call x12, Pallas kernels, run(): pl.pallas_call(kernel, out_shape=[jax.ShapeDtypeStruct(s, t) for s, t in...  74.4 us
    ppermute x8, waiting for transfers between devices, shifted(): lax.ppermute(value, CYCLE, [(i, (i + steps) % count) for i in range(count)])  53 us
    unnamed x79, local copies, waits for them, and re-layouts  37.2 us
    ppermute x8, starting transfers between devices, shifted(): lax.ppermute(value, CYCLE, [(i, (i + steps) % count) for i in range(count)])  27.6 us
    all_to_all x1, waiting for transfers between devices, per_device(): spread = lax.all_to_all(pieces, ('y', 'xl', 'xh'), 0, 0)  20.2 us
    all_to_all x1, blocking collectives, per_device(): spread = lax.all_to_all(total, 'z', 0, 0)  12.8 us
    all_gather x1, blocking collectives, per_device(): parts = lax.all_gather(total, ('xh', 'c'))  10.7 us
  transfers between devices with their start and end apart: 10, of which 5 were waited for; matrix products, arithmetic and copies ran while one was open for 1% of the time, Pallas kernels for 16%

profile of v1, /device:TPU:1, one launch (start us, length us, event | category | flops | bytes accessed | tf_op | source)
XLA Modules:
  0.0 248.9 jit_solution(6016911291251160465)
XLA Ops:
  0.6 1.3 copy-done.17
  1.9 1.3 copy-done.33
  4.5 1.5 shard_map.94
  6.0 9.8 %collective-permute-start = (bf16[528,1152]{1,0:T(8,128)(2,1)}, bf16[528,1152]{1,0:T(8,128)(2,1)}, u32[]{:S(2)}, u32[]{:S(2)}) collective-permute-start(bf16[528,1152]{1,0:T(8,128)(2,1)} %get-tuple-element.39.a0), channel_id=1, source_target_pairs={{0,252},{4,0},{8,4},{12,8},{16,12},{20,16},{24,20},{28,24},{32,28}... | collective-permute-start | bytes 3649544 | tf_op jit(solution)/shard_map/ppermute | solution.py:22
  17.6 8.9 %shard_map.95 = (f32[512,1152]{1,0:T(8,128)S(1)}, f32[512,1]{1,0:T(8,128)S(1)}, bf16[512,1152]{1,0:T(8,128)(2,1)S(1)}, bf16[1152,512]{1,0:T(8,128)(2,1)S(1)}, f3...) custom-call(f32[2]{0:T(128)S(1)} %pad_maximum_fusion.1.par, bf16[1152,1152]{1,0:T(8,128)(2,1)} %head.9, ...), custom_call_target="tpu_custom_call" | custom-call | tf_op jit(solution)/shard_map/pallas_call | solution.py:40
  26.5 1.4 copy-done
  27.9 1.0 copy-done.3
  28.9 1.4 copy-done.25
  30.3 1.4 copy-done.26
  31.7 9.9 %collective-permute-done.a1 = bf16[528,1152]{1,0:T(8,128)(2,1)} collective-permute-done((bf16[528,1152]{1,0:T(8,128)(2,1)}, bf16[528,1152]{1,0:T(8,128)(2,1)}, u32[]{:S(2)}, u32[]{:S(2)}) %collective-permute-start) | collective-permute-done | bytes 1216544 | tf_op jit(solution)/shard_map/ppermute | solution.py:22
  41.6 6.4 %collective-permute-start.1 = (bf16[528,1152]{1,0:T(8,128)(2,1)}, bf16[528,1152]{1,0:T(8,128)(2,1)}, u32[]{:S(2)}, u32[]{:S(2)}) collective-permute-start(bf16[528,1152]{1,0:T(8,128)(2,1)} %collective-permute-done.a1), channel_id=1, source_target_pairs={{0,252},{4,0},{8,4},{12,8},{16,12},{20,16},{24,20},{28,24},{32,28}... | collective-permute-start | bytes 3649544 | tf_op jit(solution)/shard_map/ppermute | solution.py:22
  48.9 12.2 %shard_map.96 = (f32[512,1152]{1,0:T(8,128)S(1)}, f32[512,1]{1,0:T(8,128)S(1)}, bf16[512,1152]{1,0:T(8,128)(2,1)S(1)}, bf16[1152,512]{1,0:T(8,128)(2,1)S(1)}, f3...) custom-call(f32[2]{0:T(128)S(1)} %pad_maximum_fusion.1.par, bf16[1152,1152]{1,0:T(8,128)(2,1)} %head.9, ...), custom_call_target="tpu_custom_call" | custom-call | tf_op jit(solution)/shard_map/pallas_call | solution.py:40
  62.0 1.4 copy-done.27
  63.4 1.4 copy-done.28
  64.8 1.0 copy-done.29
  66.5 6.3 %collective-permute-done.1.a2 = bf16[528,1152]{1,0:T(8,128)(2,1)} collective-permute-done((bf16[528,1152]{1,0:T(8,128)(2,1)}, bf16[528,1152]{1,0:T(8,128)(2,1)}, u32[]{:S(2)}, u32[]{:S(2)}) %collective-permute-start.1) | collective-permute-done | bytes 1216544 | tf_op jit(solution)/shard_map/ppermute | solution.py:22
  74.4 4.6 %collective-permute-done.4.y2 = bf16[528,1152]{1,0:T(8,128)(2,1)} collective-permute-done((bf16[528,1152]{1,0:T(8,128)(2,1)}, bf16[528,1152]{1,0:T(8,128)(2,1)}, u32[]{:S(2)}, u32[]{:S(2)}) %collective-permute-start.4) | collective-permute-done | bytes 1216544 | tf_op jit(solution)/shard_map/ppermute | solution.py:22
  78.9 1.3 copy-done.30
  82.1 14.4 %shard_map.97 = (bf16[512,1152]{1,0:T(8,128)(2,1)S(1)}, bf16[1152,512]{1,0:T(8,128)(2,1)S(1)}, bf16[512,1152]{1,0:T(8,128)(2,1)S(1)}, bf16[512,1152]{1,0:T(8,128...) custom-call(f32[2]{0:T(128)S(1)} %pad_maximum_fusion.1.par, ...), custom_call_target="tpu_custom_call" | custom-call | tf_op jit(solution)/shard_map/pallas_call | solution.py:40
  96.6 4.5 %shard_map.98 = bf16[1152,640]{1,0:T(8,128)(2,1)} custom-call(s32[1]{0:T(128)} %bitcast.5.start, bf16[1152,512]{1,0:T(8,128)(2,1)S(1)} %copy-done.4, bf16[1152,512]{1,0:T(8,128)(2,1)S(1)} %copy-done.7, bf16[1152,512]{1,0:T(8,128)(2,1)S(1)} %get-tuple-element.55.a2, bf16[512,1152]{1,0:T(8,128)(2,1)S(1)} %get-tuple-element.56.u0, ...), custom_call_target="tpu_custom_call" | custom-call | tf_op jit(solution)/shard_map/pallas_call | solution.py:40
  101.2 2.8 %collective-permute-start.8 = (bf16[1152,640]{1,0:T(8,128)(2,1)}, bf16[1152,640]{1,0:T(8,128)(2,1)}, u32[]{:S(2)}, u32[]{:S(2)}) collective-permute-start(bf16[1152,640]{1,0:T(8,128)(2,1)} %shard_map.98), channel_id=1, source_target_pairs={{0,1},{1,0},{2,3},{3,2},{4,5},{5,4},{6,7},{7,6},{8,9},{9,8},{10,11... | collective-permute-start | bytes 4423688 | tf_op jit(solution)/shard_map/ppermute | solution.py:270
  104.0 1.3 copy-done.5
  105.3 1.3 copy-done.8
  106.6 1.3 copy-done.10
  107.8 1.3 copy-done.12
  109.1 1.3 copy-done.14
  110.4 1.3 copy-done.16
  111.6 3.3 %shard_map.99.mine = f32[1152,640]{1,0:T(8,128)S(1)} custom-call(s32[1]{0:T(128)} %bitcast.4.start, bf16[1152,512]{1,0:T(8,128)(2,1)S(1)} %copy-done.5, bf16[1152,512]{1,0:T(8,128)(2,1)S(1)} %copy-done.8, bf16[1152,512]{1,0:T(8,128)(2,1)S(1)} %copy-done.10, bf16[512,1152]{1,0:T(8,128)(2,1)S(1)} %copy-done.12, bf16[512,1152]{1,0:T(8,128)(2,1)S(1)} %copy-done.14, ...), custom_call_target="tpu_custom_call" | custom-call | tf_op jit(solution)/shard_map/pallas_call | solution.py:40
  114.9 3.4 %shard_map.100.gy0 = f32[512,1152]{1,0:T(8,128)S(1)} custom-call(f32[2]{0:T(128)S(1)} %pad_maximum_fusion.1.par, bf16[528,1152]{1,0:T(8,128)(2,1)S(1)} %get-tuple-element.40.y0, bf16[528,1152]{1,0:T(8,128)(2,1)} %collective-permute-done.1.a2, bf16[512,1152]{1,0:T(8,128)(2,1)S(1)} %copy-done.32, f32[512,1]{1,0:T(8,128)S(1)} %copy.23.tid, ...), custom_call_target="tpu_custom_call" | custom-call | tf_op jit(solution)/shard_map/pallas_call | solution.py:40
  118.3 1.4 copy-done.1
  119.7 1.7 shard_map.101
  121.4 1.3 copy-done.2
  122.7 4.4 %all-to-all-start = ((bf16[16,144,384]{2,1,0:T(8,128)(2,1)}), bf16[16,144,384]{2,1,0:T(8,128)(2,1)}, u32[]{:S(2)}, u32[]{:S(2)}) async-start(bf16[16,144,384]{2,1,0:T(8,128)(2,1)} %copy-done.2), calls=%async_computation | async-start | bytes 3538944 | tf_op jit(solution)/shard_map/all_to_all | solution.py:277
  127.3 5.7 %collective-permute-start.3 = (bf16[528,1152]{1,0:T(8,128)(2,1)}, bf16[528,1152]{1,0:T(8,128)(2,1)}, u32[]{:S(2)}, u32[]{:S(2)}) collective-permute-start(bf16[528,1152]{1,0:T(8,128)(2,1)} %collective-permute-done.1.a2), channel_id=1, source_target_pairs={{0,252},{4,0},{8,4},{12,8},{16,12},{20,16},{24,20},{28,24},{32,28}... | collective-permute-start | bytes 3649544 | tf_op jit(solution)/shard_map/ppermute | solution.py:22
  132.9 32.3 %collective-permute-done.6.y3 = bf16[528,1152]{1,0:T(8,128)(2,1)} collective-permute-done((bf16[528,1152]{1,0:T(8,128)(2,1)}, bf16[528,1152]{1,0:T(8,128)(2,1)}, u32[]{:S(2)}, u32[]{:S(2)}) %collective-permute-start.6) | collective-permute-done | bytes 1216544 | tf_op jit(solution)/shard_map/ppermute | solution.py:22
  165.2 5.7 %collective-permute-start.5 = (bf16[528,1152]{1,0:T(8,128)(2,1)}, bf16[528,1152]{1,0:T(8,128)(2,1)}, u32[]{:S(2)}, u32[]{:S(2)}) collective-permute-start(bf16[528,1152]{1,0:T(8,128)(2,1)} %collective-permute-done.3.a3), channel_id=1, source_target_pairs={{0,252},{4,0},{8,4},{12,8},{16,12},{20,16},{24,20},{28,24},{32,28}... | collective-permute-start | bytes 3649544 | tf_op jit(solution)/shard_map/ppermute | solution.py:22
  170.9 1.7 copy-done.24
  172.5 9.2 %shard_map.102 = (f32[512,1152]{1,0:T(8,128)S(1)}, f32[512,1152]{1,0:T(8,128)S(1)}, bf16[512,1152]{1,0:T(8,128)(2,1)}) custom-call(f32[2]{0:T(128)S(1)} %pad_maximum_fusion.1.par, bf16[1152,1152]{1,0:T(8,128)(2,1)} %head.9, bf16[528,1152]{1,0:T(8,128)(2,1)} %collective-permute-done.3.a3, bf16[528,1152]{1,0:T(8,128)(2,1)} %collective-permute-done.6.y3, ...), custom_call_target="tpu_custom_call" | custom-call | tf_op jit(solution)/shard_map/pallas_call | solution.py:40
  181.8 1.4 copy-done.19
  183.2 1.5 copy-done.21
  184.6 20.2 %all-to-all-done.got = bf16[16,144,384]{2,1,0:T(8,128)(2,1)} async-done(((bf16[16,144,384]{2,1,0:T(8,128)(2,1)}), bf16[16,144,384]{2,1,0:T(8,128)(2,1)}, u32[]{:S(2)}, u32[]{:S(2)}) %all-to-all-start) | async-done | bytes 1769504 | tf_op jit(solution)/shard_map/all_to_all | solution.py:277
  204.8 1.7 shard_map.103
  206.6 12.8 %all_to_all.10.got = f32[8,18,384]{2,1,0:T(8,128)S(1)} all-to-all(f32[8,18,384]{2,1,0:T(8,128)S(1)} %shard_map.103), channel_id=1, replica_groups=mesh['y'=4,'xl'=2,'z'=8,'xh'=2,'c'=2] {'z'}, dimensions={0} | all-to-all | bytes 442368 | tf_op jit(solution)/shard_map/all_to_all | solution.py:284
  219.4 10.7 %all-gather.1 = f32[4,18,384]{2,1,0:T(8,128)S(1)} all-gather(f32[1,18,384]{2,1,0:T(8,128)S(1)} %bitcast.13), channel_id=2, replica_groups=mesh['y'=4,'xl'=2,'z'=8,'xh'=2,'c'=2] {'xh','c'}, dimensions={0}, use_global_device_ids=true | all-gather | bytes 138240 | tf_op jit(solution)/shard_map/all_gather | solution.py:286
  230.8 1.3 copy-done.18
  232.0 1.7 copy-done.20
  233.7 1.7 copy-done.22
  235.4 13.6 %shard_map.105 = (bf16[512,1152]{1,0:T(8,128)(2,1)}, bf16[512,1152]{1,0:T(8,128)(2,1)}, bf16[512,1152]{1,0:T(8,128)(2,1)}) custom-call(f32[2]{0:T(128)S(1)} %pad_maximum_fusion.1.par, bf16[1152,1152]{1,0:T(8,128)(2,1)} %head.9, bf16[528,1152]{1,0:T(8,128)(2,1)} %collective-permute-done.5.a4, bf16[528,1152]{1,0:T(8,128)(2,1)} %collective-permute-done.7.y4, ...), custom_call_target="tpu_custom_call" | custom-call | tf_op jit(solution)/shard_map/pallas_call | solution.py:40
  (79 shorter events, 8.7 us)
Async XLA Ops:
  0.6 1.3 copy-start.17
  1.9 1.3 copy-start.33
  3.2 0.7 copy-start.37
  6.0 35.5 %collective-permute-start = (bf16[528,1152]{1,0:T(8,128)(2,1)}, bf16[528,1152]{1,0:T(8,128)(2,1)}, u32[]{:S(2)}, u32[]{:S(2)}) collective-permute-start(bf16[528,1152]{1,0:T(8,128)(2,1)} %get-tuple-element.39.a0), channel_id=1, source_target_pairs={{0,252},{4,0},{8,4},{12,8},{16,12},{20,16},{24,20},{28,24},{32,28}... | collective-permute-start | bytes 3649544 | tf_op jit(solution)/shard_map/ppermute | solution.py:22
  15.8 32.2 %collective-permute-start.2 = (bf16[528,1152]{1,0:T(8,128)(2,1)S(1)}, bf16[528,1152]{1,0:T(8,128)(2,1)}, u32[]{:S(2)}, u32[]{:S(2)}) collective-permute-start(bf16[528,1152]{1,0:T(8,128)(2,1)S(1)} %get-tuple-element.40.y0), channel_id=1, source_target_pairs={{0,4},{4,8},{8,12},{12,16},{16,20},{20,24},{24,28},{28,32},{32,36}... | collective-permute-start | bytes 3649544 | tf_op jit(solution)/shard_map/ppermute | solution.py:22
  26.5 1.4 copy-start
  27.9 1.0 copy-start.3
  28.9 1.4 copy-start.25
  30.3 1.4 copy-start.26
  41.6 31.2 %collective-permute-start.1 = (bf16[528,1152]{1,0:T(8,128)(2,1)}, bf16[528,1152]{1,0:T(8,128)(2,1)}, u32[]{:S(2)}, u32[]{:S(2)}) collective-permute-start(bf16[528,1152]{1,0:T(8,128)(2,1)} %collective-permute-done.a1), channel_id=1, source_target_pairs={{0,252},{4,0},{8,4},{12,8},{16,12},{20,16},{24,20},{28,24},{32,28}... | collective-permute-start | bytes 3649544 | tf_op jit(solution)/shard_map/ppermute | solution.py:22
  48.0 31.0 %collective-permute-start.4 = (bf16[528,1152]{1,0:T(8,128)(2,1)}, bf16[528,1152]{1,0:T(8,128)(2,1)}, u32[]{:S(2)}, u32[]{:S(2)}) collective-permute-start(bf16[528,1152]{1,0:T(8,128)(2,1)} %collective-permute-done.2.y1), channel_id=1, source_target_pairs={{0,4},{4,8},{8,12},{12,16},{16,20},{20,24},{24,28},{28,32},{32,36}... | collective-permute-start | bytes 3649544 | tf_op jit(solution)/shard_map/ppermute | solution.py:22
  61.0 1.0 copy-start.6
  62.0 1.4 copy-start.27
  63.4 1.4 copy-start.28
  64.8 1.0 copy-start.29
  65.8 0.7 copy-start.35
  78.9 1.3 copy-start.30
  80.2 0.9 copy-start.34
  81.2 0.9 copy-start.36
  82.1 14.5 %copy-start.4 = (bf16[1152,512]{1,0:T(8,128)(2,1)S(1)}, bf16[1152,512]{1,0:T(8,128)(2,1)}, u32[]{:S(2)}) copy-start(bf16[1152,512]{1,0:T(8,128)(2,1)} %copy-done.3) | copy-start | bytes 3538948
  82.1 14.5 %copy-start.7 = (bf16[1152,512]{1,0:T(8,128)(2,1)S(1)}, bf16[1152,512]{1,0:T(8,128)(2,1)}, u32[]{:S(2)}) copy-start(bf16[1152,512]{1,0:T(8,128)(2,1)} %copy-done.6) | copy-start | bytes 3538948
  96.6 4.6 %copy-start.9 = (bf16[1152,512]{1,0:T(8,128)(2,1)}, bf16[1152,512]{1,0:T(8,128)(2,1)S(1)}, u32[]{:S(2)}) copy-start(bf16[1152,512]{1,0:T(8,128)(2,1)S(1)} %get-tuple-element.55.a2) | copy-start | bytes 3538948
  96.6 4.6 %copy-start.11 = (bf16[512,1152]{1,0:T(8,128)(2,1)}, bf16[512,1152]{1,0:T(8,128)(2,1)S(1)}, u32[]{:S(2)}) copy-start(bf16[512,1152]{1,0:T(8,128)(2,1)S(1)} %get-tuple-element.56.u0) | copy-start | bytes 3538948
  96.6 4.6 %copy-start.13 = (bf16[512,1152]{1,0:T(8,128)(2,1)}, bf16[512,1152]{1,0:T(8,128)(2,1)S(1)}, u32[]{:S(2)}) copy-start(bf16[512,1152]{1,0:T(8,128)(2,1)S(1)} %get-tuple-element.57.u1) | copy-start | bytes 3538948
  96.6 4.6 %copy-start.15 = (bf16[512,1152]{1,0:T(8,128)(2,1)}, bf16[512,1152]{1,0:T(8,128)(2,1)S(1)}, u32[]{:S(2)}) copy-start(bf16[512,1152]{1,0:T(8,128)(2,1)S(1)} %get-tuple-element.58.u2) | copy-start | bytes 3538948
  96.6 4.6 %copy-start.31 = (bf16[512,1152]{1,0:T(8,128)(2,1)}, bf16[512,1152]{1,0:T(8,128)(2,1)S(1)}, u32[]{:S(2)}) copy-start(bf16[512,1152]{1,0:T(8,128)(2,1)S(1)} %get-tuple-element.64.x2) | copy-start | bytes 3538948
  101.2 18.5 %collective-permute-start.8 = (bf16[1152,640]{1,0:T(8,128)(2,1)}, bf16[1152,640]{1,0:T(8,128)(2,1)}, u32[]{:S(2)}, u32[]{:S(2)}) collective-permute-start(bf16[1152,640]{1,0:T(8,128)(2,1)} %shard_map.98), channel_id=1, source_target_pairs={{0,1},{1,0},{2,3},{3,2},{4,5},{5,4},{6,7},{7,6},{8,9},{9,8},{10,11... | collective-permute-start | bytes 4423688 | tf_op jit(solution)/shard_map/ppermute | solution.py:270
  104.0 1.3 copy-start.5
  105.3 1.3 copy-start.8
  106.6 1.3 copy-start.10
  107.8 1.3 copy-start.12
  109.1 1.3 copy-start.14
  110.4 1.3 copy-start.16
  111.6 3.3 %copy-start.23 = (f32[512,1152]{1,0:T(8,128)S(1)}, f32[512,1152]{1,0:T(8,128)}, u32[]{:S(2)}) copy-start(f32[512,1152]{1,0:T(8,128)} %get-tuple-element.66.gy0) | copy-start | bytes 7077892
  111.6 3.3 %copy-start.32 = (bf16[512,1152]{1,0:T(8,128)(2,1)S(1)}, bf16[512,1152]{1,0:T(8,128)(2,1)}, u32[]{:S(2)}) copy-start(bf16[512,1152]{1,0:T(8,128)(2,1)} %copy-done.31) | copy-start | bytes 3538948
  118.3 1.4 copy-start.1
  121.4 1.3 copy-start.2
  122.7 82.1 %all-to-all-start = ((bf16[16,144,384]{2,1,0:T(8,128)(2,1)}), bf16[16,144,384]{2,1,0:T(8,128)(2,1)}, u32[]{:S(2)}, u32[]{:S(2)}) async-start(bf16[16,144,384]{2,1,0:T(8,128)(2,1)} %copy-done.2), calls=%async_computation | async-start | bytes 3538944 | tf_op jit(solution)/shard_map/all_to_all | solution.py:277
  127.2 38.0 %collective-permute-start.6 = (bf16[528,1152]{1,0:T(8,128)(2,1)}, bf16[528,1152]{1,0:T(8,128)(2,1)}, u32[]{:S(2)}, u32[]{:S(2)}) collective-permute-start(bf16[528,1152]{1,0:T(8,128)(2,1)} %collective-permute-done.4.y2), channel_id=1, source_target_pairs={{0,4},{4,8},{8,12},{12,16},{16,20},{20,24},{24,28},{28,32},{32,36}... | collective-permute-start | bytes 3649544 | tf_op jit(solution)/shard_map/ppermute | solution.py:22
  127.3 37.9 %collective-permute-start.3 = (bf16[528,1152]{1,0:T(8,128)(2,1)}, bf16[528,1152]{1,0:T(8,128)(2,1)}, u32[]{:S(2)}, u32[]{:S(2)}) collective-permute-start(bf16[528,1152]{1,0:T(8,128)(2,1)} %collective-permute-done.1.a2), channel_id=1, source_target_pairs={{0,252},{4,0},{8,4},{12,8},{16,12},{20,16},{24,20},{28,24},{32,28}... | collective-permute-start | bytes 3649544 | tf_op jit(solution)/shard_map/ppermute | solution.py:22
  165.2 65.6 %collective-permute-start.7 = (bf16[528,1152]{1,0:T(8,128)(2,1)}, bf16[528,1152]{1,0:T(8,128)(2,1)}, u32[]{:S(2)}, u32[]{:S(2)}) collective-permute-start(bf16[528,1152]{1,0:T(8,128)(2,1)} %collective-permute-done.6.y3), channel_id=1, source_target_pairs={{0,4},{4,8},{8,12},{12,16},{16,20},{20,24},{24,28},{28,32},{32,36}... | collective-permute-start | bytes 3649544 | tf_op jit(solution)/shard_map/ppermute | solution.py:22
  165.2 65.6 %collective-permute-start.5 = (bf16[528,1152]{1,0:T(8,128)(2,1)}, bf16[528,1152]{1,0:T(8,128)(2,1)}, u32[]{:S(2)}, u32[]{:S(2)}) collective-permute-start(bf16[528,1152]{1,0:T(8,128)(2,1)} %collective-permute-done.3.a3), channel_id=1, source_target_pairs={{0,252},{4,0},{8,4},{12,8},{16,12},{20,16},{24,20},{28,24},{32,28}... | collective-permute-start | bytes 3649544 | tf_op jit(solution)/shard_map/ppermute | solution.py:22
  170.9 1.7 copy-start.24
  181.8 1.4 copy-start.19
  183.2 1.5 copy-start.21
  230.8 1.3 copy-start.18
  232.0 1.7 copy-start.20
  233.7 1.7 copy-start.22
  (1 other events, 0.7 us)

commit v2 on v1

--- a/solution.py
+++ b/solution.py
@@ -34,7 +34,7 @@
     return lax.dot_general(a, b, (((1,), (1,)), ((), ())), preferred_element_type=F32)
 
 
-def run(kernel, outs, *args, scalars=1, aliases=None, vmem=40):
+def run(kernel, outs, *args, scalars=1, aliases=None, vmem=14, flops=0):
     specs = [pl.BlockSpec(memory_space=pltpu.SMEM)] * scalars
     specs += [pl.BlockSpec(memory_space=pltpu.VMEM)] * (len(args) - scalars)
     return pl.pallas_call(
@@ -44,7 +44,7 @@
         out_specs=[pl.BlockSpec(memory_space=pltpu.VMEM)] * len(outs),
         input_output_aliases=aliases or {},
         compiler_params=pltpu.CompilerParams(vmem_limit_bytes=vmem * 2**20),
-        cost_estimate=pl.CostEstimate(flops=0, bytes_accessed=0, transcendentals=0),
+        cost_estimate=pl.CostEstimate(flops=flops, bytes_accessed=0, transcendentals=0),
     )(*args)
 
 
@@ -153,16 +153,20 @@
     steps(body)
 
 
-def head_part(start, a0, a1, a2, u0, u1, u2, out):
+def head_part(start, a0, a1, a2, u0, u1, u2, *outs):
     cols = pl.ds(pl.multiple_of(start[0], 128), WIDE)
 
-    @pl.loop(0, D // 384)
-    def _(k):
-        r = pl.ds(pl.multiple_of(k * 384, 384), 384)
-        total = nn(a0[r, :], u0[:, cols])
-        total = total + nn(a1[r, :], u1[:, cols])
-        total = total + nn(a2[r, :], u2[:, cols])
-        out[r, :] = total.astype(out.dtype)
+    for i, out in enumerate(outs):
+
+        @pl.loop(0, D // 288 // len(outs))
+        def _(k):
+            at = pl.multiple_of(k * 288, 288)
+            s = pl.ds(at, 288)
+            r = pl.ds(at + D // len(outs) * i, 288)
+            total = nn(a0[r, :], u0[:, cols])
+            total = total + nn(a1[r, :], u1[:, cols])
+            total = total + nn(a2[r, :], u2[:, cols])
+            out[s, :] = total.astype(out.dtype)
 
 
 def text_only(par, y0, a2, x2, tid, gy0, gy):
@@ -174,11 +178,19 @@
     steps(body)
 
 
-def to_pieces(mine, away, out):
-    @pl.loop(0, 8)
+def to_pieces(mine, low, high, out):
+    @pl.loop(0, 4)
     def _(k):
         r = pl.ds(pl.multiple_of(k * 144, 144), 144)
-        total = (mine[r, :] + away[r, :].astype(F32)).astype(BF16)
+        total = (mine[r, :] + low[r, :].astype(F32)).astype(BF16)
+        out[2 * k] = total[:, :PART]
+        out[2 * k + 1] = total[:, 256 : 256 + PART]
+
+    @pl.loop(4, 8)
+    def _(k):
+        r = pl.ds(pl.multiple_of(k * 144, 144), 144)
+        s = pl.ds(pl.multiple_of((k - 4) * 144, 144), 144)
+        total = (mine[r, :] + high[s, :].astype(F32)).astype(BF16)
         out[2 * k] = total[:, :PART]
         out[2 * k + 1] = total[:, 256 : 256 + PART]
 
@@ -265,19 +277,19 @@
         third, [BLOCK, TURNED, BLOCK, BLOCK, BLOCK, WIDEBLOCK, WIDEBLOCK, COLUMN],
         par, head, a2, y2, x0, f0, v0, x1, f1, v1, iid, column_ids(a1), column_ids(a2), gx,
     )
-    half = ((D, WIDE), BF16)
-    (away,) = run(head_part, [half], (512 * (1 - core)).reshape(1), at0, at1, at2, u0, u1, u2)
-    got = lax.ppermute(away, "c", [(0, 1), (1, 0)])
+    half = ((D // 2, WIDE), BF16)
+    away = run(head_part, [half, half], (512 * (1 - core)).reshape(1), at0, at1, at2, u0, u1, u2)
+    got = [lax.ppermute(part, "c", [(0, 1), (1, 0)]) for part in away]
     (mine,) = run(
         head_part, [((D, WIDE), F32)],
-        after((512 * core).reshape(1), away), at0, at1, at2, u0, u1, u2,
+        after((512 * core).reshape(1), *away), at0, at1, at2, u0, u1, u2,
     )
     (gy,) = run(text_only, [WIDEBLOCK], par, y0, a2, x2, tid, after(gy, mine))
-    (pieces,) = run(to_pieces, [((16, 144, PART), BF16)], after(mine, gy), got, scalars=0)
+    (pieces,) = run(to_pieces, [((16, 144, PART), BF16)], after(mine, gy), *got, scalars=0)
     spread = lax.all_to_all(pieces, ("y", "xl", "xh"), 0, 0)
     gx, gy, _ = run(
         fourth, [WIDEBLOCK, WIDEBLOCK, BLOCK],
-        par, head, a3, y3, x0, y0, iid, tid, gx, after(gy, pieces),
+        par, head, a3, y3, x0, y0, iid, tid, gx, after(gy, pieces), flops=10**11,
     )
     y4, a4 = shifted(after(y3, mine), 1), shifted(after(a3, mine), -1)
     (total,) = run(add_pieces, [((8, 18, PART), F32)], after(spread, gx), scalars=0)

time: 250 us -> 236 us (0.944)
  waiting for transfers between devices: 73.2 us -> 43 us
  local copies, waits for them, and re-layouts: 38.5 us -> 62.6 us
  Pallas kernels: 74.4 us -> 66.4 us
    ppermute x8, waiting for transfers between devices: 53 us -> 14.9 us  [shifted(): lax.ppermute(value, CYCLE, [(i, (i + steps) % count) for i in range(count)])]
    unnamed x79 -> x111, local copies, waits for them, and re-layouts: 37.2 us -> 59.8 us
    pallas_call x12, Pallas kernels: 74.4 us -> 66.4 us  [run(): pl.pallas_call(kernel, out_shape=[jax.ShapeDtypeStruct(s, t) for s, t in...]
    all_to_all x1, waiting for transfers between devices: 20.2 us -> 28 us  [per_device(): spread = lax.all_to_all(pieces, ('y', 'xl', 'xh'), 0, 0)]
  transfers between devices with their start and end apart: 10 -> 11, of which waited for: 5 -> 3; matrix products, arithmetic and copies ran while one was open for 1% -> 3% of each run, Pallas kernels for 16% -> 22%
where the time goes in v2:
time: 236 us; the launch traced here: 234 us
  Pallas kernels  66.4 us (28%)
  local copies, waits for them, and re-layouts  62.6 us (27%)
  waiting for transfers between devices  43 us (18%)
  starting transfers between devices  34.2 us (14%)
  blocking collectives  23.2 us (10%)
    pallas_call x12, Pallas kernels, run(): pl.pallas_call(kernel, out_shape=[jax.ShapeDtypeStruct(s, t) for s, t in...  66.4 us
    unnamed x111, local copies, waits for them, and re-layouts  59.8 us
    all_to_all x1, waiting for transfers between devices, per_device(): spread = lax.all_to_all(pieces, ('y', 'xl', 'xh'), 0, 0)  28 us
    ppermute x8, starting transfers between devices, shifted(): lax.ppermute(value, CYCLE, [(i, (i + steps) % count) for i in range(count)])  26.9 us
    ppermute x8, waiting for transfers between devices, shifted(): lax.ppermute(value, CYCLE, [(i, (i + steps) % count) for i in range(count)])  14.9 us
    all_to_all x1, blocking collectives, per_device(): spread = lax.all_to_all(total, 'z', 0, 0)  12.9 us
    all_gather x1, blocking collectives, per_device(): parts = lax.all_gather(total, ('xh', 'c'))  10.2 us
  transfers between devices with their start and end apart: 11, of which 3 were waited for; matrix products, arithmetic and copies ran while one was open for 3% of the time, Pallas kernels for 22%

profile of v2, /device:TPU:1, one launch (start us, length us, event | category | flops | bytes accessed | tf_op | source)
XLA Modules:
  0.0 233.7 jit_solution(5424219016197719155)
XLA Ops:
  1.9 1.3 copy-done.46
  4.5 2.0 shard_map.94
  6.5 2.5 %collective-permute-start.2 = (bf16[528,1152]{1,0:T(8,128)(2,1)}, bf16[528,1152]{1,0:T(8,128)(2,1)}, u32[]{:S(2)}, u32[]{:S(2)}) collective-permute-start(bf16[528,1152]{1,0:T(8,128)(2,1)} %get-tuple-element.42.y0), channel_id=1, source_target_pairs={{0,4},{4,8},{8,12},{12,16},{16,20},{20,24},{24,28},{28,32},{32,36}... | collective-permute-start | bytes 3649544 | tf_op jit(solution)/shard_map/ppermute | solution.py:22
  9.0 7.3 %collective-permute-start = (bf16[528,1152]{1,0:T(8,128)(2,1)}, bf16[528,1152]{1,0:T(8,128)(2,1)}, u32[]{:S(2)}, u32[]{:S(2)}) collective-permute-start(bf16[528,1152]{1,0:T(8,128)(2,1)} %get-tuple-element.41.a0), channel_id=1, source_target_pairs={{0,252},{4,0},{8,4},{12,8},{16,12},{20,16},{24,20},{28,24},{32,28}... | collective-permute-start | bytes 3649544 | tf_op jit(solution)/shard_map/ppermute | solution.py:22
  18.0 8.5 %shard_map.95 = (f32[512,1152]{1,0:T(8,128)S(1)}, f32[512,1]{1,0:T(8,128)S(1)}, bf16[512,1152]{1,0:T(8,128)(2,1)S(1)}, bf16[1152,512]{1,0:T(8,128)(2,1)S(1)}, f3...) custom-call(f32[2]{0:T(128)S(1)} %pad_maximum_fusion.1.par, bf16[1152,1152]{1,0:T(8,128)(2,1)S(1)} %copy-done, ...), custom_call_target="tpu_custom_call" | custom-call | tf_op jit(solution)/shard_map/pallas_call | solution.py:40
  27.6 1.4 copy-done.6
  30.0 1.4 copy-done.38
  31.4 1.4 copy-done.40
  32.8 10.3 %collective-permute-done.2.y1 = bf16[528,1152]{1,0:T(8,128)(2,1)} collective-permute-done((bf16[528,1152]{1,0:T(8,128)(2,1)}, bf16[528,1152]{1,0:T(8,128)(2,1)}, u32[]{:S(2)}, u32[]{:S(2)}) %collective-permute-start.2) | collective-permute-done | bytes 1216544 | tf_op jit(solution)/shard_map/ppermute | solution.py:22
  43.1 5.7 %collective-permute-start.1 = (bf16[528,1152]{1,0:T(8,128)(2,1)}, bf16[528,1152]{1,0:T(8,128)(2,1)}, u32[]{:S(2)}, u32[]{:S(2)}) collective-permute-start(bf16[528,1152]{1,0:T(8,128)(2,1)} %collective-permute-done.a1), channel_id=1, source_target_pairs={{0,252},{4,0},{8,4},{12,8},{16,12},{20,16},{24,20},{28,24},{32,28}... | collective-permute-start | bytes 3649544 | tf_op jit(solution)/shard_map/ppermute | solution.py:22
  48.8 1.3 copy-done.2
  50.1 1.7 copy-done.39
  51.7 1.7 copy-done.41
  53.4 8.9 %shard_map.96 = (f32[512,1152]{1,0:T(8,128)S(1)}, f32[512,1]{1,0:T(8,128)S(1)}, bf16[512,1152]{1,0:T(8,128)(2,1)S(1)}, bf16[1152,512]{1,0:T(8,128)(2,1)S(1)}, f3...) custom-call(f32[2]{0:T(128)S(1)} %pad_maximum_fusion.1.par, bf16[1152,1152]{1,0:T(8,128)(2,1)S(1)} %copy-done, ...), custom_call_target="tpu_custom_call" | custom-call | tf_op jit(solution)/shard_map/pallas_call | solution.py:40
  63.3 1.4 copy-done.30
  64.7 1.4 copy-done.34
  66.1 1.5 copy-done.36
  70.0 4.6 %collective-permute-done.4.y2 = bf16[528,1152]{1,0:T(8,128)(2,1)} collective-permute-done((bf16[528,1152]{1,0:T(8,128)(2,1)}, bf16[528,1152]{1,0:T(8,128)(2,1)}, u32[]{:S(2)}, u32[]{:S(2)}) %collective-permute-start.4) | collective-permute-done | bytes 1216544 | tf_op jit(solution)/shard_map/ppermute | solution.py:22
  74.7 5.7 %collective-permute-start.3 = (bf16[528,1152]{1,0:T(8,128)(2,1)}, bf16[528,1152]{1,0:T(8,128)(2,1)}, u32[]{:S(2)}, u32[]{:S(2)}) collective-permute-start(bf16[528,1152]{1,0:T(8,128)(2,1)} %collective-permute-done.1.a2), channel_id=1, source_target_pairs={{0,252},{4,0},{8,4},{12,8},{16,12},{20,16},{24,20},{28,24},{32,28}... | collective-permute-start | bytes 3649544 | tf_op jit(solution)/shard_map/ppermute | solution.py:22
  82.8 1.3 copy-done.3
  84.1 1.7 copy-done.7
  85.8 1.7 copy-done.35
  87.4 1.7 copy-done.37
  89.1 1.3 copy-done.43
  93.2 11.8 %shard_map.97 = (bf16[512,1152]{1,0:T(8,128)(2,1)S(1)}, bf16[1152,512]{1,0:T(8,128)(2,1)S(1)}, bf16[512,1152]{1,0:T(8,128)(2,1)S(1)}, bf16[512,1152]{1,0:T(8,128...) custom-call(f32[2]{0:T(128)S(1)} %pad_maximum_fusion.1.par, ...), custom_call_target="tpu_custom_call" | custom-call | tf_op jit(solution)/shard_map/pallas_call | solution.py:40
  105.0 1.4 copy-done.53
  106.5 4.4 %shard_map.98 = (bf16[576,640]{1,0:T(8,128)(2,1)}, bf16[576,640]{1,0:T(8,128)(2,1)}) custom-call(s32[1]{0:T(128)} %bitcast.5.start, bf16[1152,512]{1,0:T(8,128)(2,1)S(1)} %copy-done.11, bf16[1152,512]{1,0:T(8,128)(2,1)S(1)} %copy-done.14, bf16[1152,512]{1,0:T(8,128)(2,1)S(1)} %get-tuple-element.57.a2, bf16[512,1152]{1,0:T(8,128)(2,1)S(1)} %get-tuple-element.58.u0, ...), custom_call_target="tpu_custom_call" | custom-call | tf_op jit(solution)/shard_map/pallas_call | solution.py:40
  110.9 2.8 %collective-permute-start.8 = (bf16[576,640]{1,0:T(8,128)(2,1)}, bf16[576,640]{1,0:T(8,128)(2,1)}, u32[]{:S(2)}, u32[]{:S(2)}) collective-permute-start(bf16[576,640]{1,0:T(8,128)(2,1)} %get-tuple-element.61), channel_id=1, source_target_pairs={{0,1},{1,0},{2,3},{3,2},{4,5},{5,4},{6,7},{7,6},{8,9},{9,8},{10,11... | collective-permute-start | bytes 2211848 | tf_op jit(solution)/shard_map/ppermute | solution.py:282
  113.7 1.3 copy-done.12
  121.4 3.4 %shard_map.99.mine = f32[1152,640]{1,0:T(8,128)S(1)} custom-call(s32[1]{0:T(128)} %bitcast.4.start, bf16[1152,512]{1,0:T(8,128)(2,1)S(1)} %copy-done.12, bf16[1152,512]{1,0:T(8,128)(2,1)S(1)} %copy-done.15, bf16[1152,512]{1,0:T(8,128)(2,1)S(1)} %copy-done.17, bf16[512,1152]{1,0:T(8,128)(2,1)S(1)} %copy-done.19, bf16[512,1152]{1,0:T(8,128)(2,1)S(1)} %copy-done.21, ...), custom_call_target="tpu_custom_call" | custom-call | tf_op jit(solution)/shard_map/pallas_call | solution.py:40
  124.8 3.7 %shard_map.100.gy0 = f32[512,1152]{1,0:T(8,128)S(1)} custom-call(f32[2]{0:T(128)S(1)} %pad_maximum_fusion.1.par, bf16[528,1152]{1,0:T(8,128)(2,1)} %get-tuple-element.42.y0, bf16[528,1152]{1,0:T(8,128)(2,1)} %collective-permute-done.1.a2, bf16[512,1152]{1,0:T(8,128)(2,1)S(1)} %copy-done.45, f32[512,1]{1,0:T(8,128)S(1)} %copy.23.tid, f32[512,1152]{1,0:T(8,128)S(1)} %copy-done.31), custom_call_target="tpu_custom_call" | custom-call | tf_op jit(solution)/shard_map/pallas_call | solution.py:40
  128.5 1.4 copy-done.32
  130.0 1.7 shard_map.101
  132.9 4.4 %all-to-all-start = ((bf16[16,144,384]{2,1,0:T(8,128)(2,1)}), bf16[16,144,384]{2,1,0:T(8,128)(2,1)}, u32[]{:S(2)}, u32[]{:S(2)}) async-start(bf16[16,144,384]{2,1,0:T(8,128)(2,1)} %copy-done.9), calls=%async_computation | async-start | bytes 3538944 | tf_op jit(solution)/shard_map/all_to_all | solution.py:289
  137.4 5.7 %collective-permute-start.5 = (bf16[528,1152]{1,0:T(8,128)(2,1)}, bf16[528,1152]{1,0:T(8,128)(2,1)}, u32[]{:S(2)}, u32[]{:S(2)}) collective-permute-start(bf16[528,1152]{1,0:T(8,128)(2,1)} %collective-permute-done.3.a3), channel_id=1, source_target_pairs={{0,252},{4,0},{8,4},{12,8},{16,12},{20,16},{24,20},{28,24},{32,28}... | collective-permute-start | bytes 3649544 | tf_op jit(solution)/shard_map/ppermute | solution.py:22
  144.4 1.7 copy-done.33
  146.0 1.7 copy-done.54
  147.7 8.0 %shard_map.102 = (f32[512,1152]{1,0:T(8,128)S(1)}, f32[512,1152]{1,0:T(8,128)S(1)}, bf16[512,1152]{1,0:T(8,128)(2,1)}) custom-call(f32[2]{0:T(128)S(1)} %pad_maximum_fusion.1.par, bf16[1152,1152]{1,0:T(8,128)(2,1)S(1)} %copy-done, bf16[528,1152]{1,0:T(8,128)(2,1)} %collective-permute-done.3.a3, bf16[528,1152]{1,0:T(8,128)(2,1)} %collective-permute-done.6.y3, ...), custom_call_target="tpu_custom_call" | custom-call | flops 99999997952 | tf_op jit(solution)/shard_map/pallas_call | solution.py:40
  155.7 1.4 copy-done.26
  157.1 1.4 copy-done.28
  158.5 28.0 %all-to-all-done.got = bf16[16,144,384]{2,1,0:T(8,128)(2,1)} async-done(((bf16[16,144,384]{2,1,0:T(8,128)(2,1)}), bf16[16,144,384]{2,1,0:T(8,128)(2,1)}, u32[]{:S(2)}, u32[]{:S(2)}) %all-to-all-start) | async-done | bytes 1769504 | tf_op jit(solution)/shard_map/all_to_all | solution.py:289
  186.5 1.7 shard_map.103
  188.2 12.9 %all_to_all.10.got = f32[8,18,384]{2,1,0:T(8,128)S(1)} all-to-all(f32[8,18,384]{2,1,0:T(8,128)S(1)} %shard_map.103), channel_id=1, replica_groups=mesh['y'=4,'xl'=2,'z'=8,'xh'=2,'c'=2] {'z'}, dimensions={0} | all-to-all | bytes 442368 | tf_op jit(solution)/shard_map/all_to_all | solution.py:296
  201.2 10.2 %all-gather.1 = f32[4,18,384]{2,1,0:T(8,128)} all-gather(f32[1,18,384]{2,1,0:T(8,128)S(1)} %bitcast.13), channel_id=2, replica_groups=mesh['y'=4,'xl'=2,'z'=8,'xh'=2,'c'=2] {'xh','c'}, dimensions={0}, use_global_device_ids=true | all-gather | bytes 138240 | tf_op jit(solution)/shard_map/all_gather | solution.py:298
  215.1 1.7 copy-done.8
  218.0 1.7 copy-done.27
  219.7 1.7 copy-done.29
  221.3 12.4 %shard_map.105 = (bf16[512,1152]{1,0:T(8,128)(2,1)}, bf16[512,1152]{1,0:T(8,128)(2,1)}, bf16[512,1152]{1,0:T(8,128)(2,1)}) custom-call(f32[2]{0:T(128)S(1)} %pad_maximum_fusion.1.par, bf16[1152,1152]{1,0:T(8,128)(2,1)S(1)} %copy-done, bf16[528,1152]{1,0:T(8,128)(2,1)} %collective-permute-done.5.a4, bf16[528,1152]{1,0:T(8,128)(2,1)} %collective-permute-done.7.y4, ...), custom_call_target="tpu_custom_call" | custom-call | tf_op jit(solution)/shard_map/pallas_call | solution.py:40
  (113 shorter events, 27.9 us)
Async XLA Ops:
  0.6 1.3 copy-start.24
  4.5 13.5 %copy-start = (bf16[1152,1152]{1,0:T(8,128)(2,1)S(1)}, bf16[1152,1152]{1,0:T(8,128)(2,1)}, u32[]{:S(2)}) copy-start(bf16[1152,1152]{1,0:T(8,128)(2,1)} %head.9) | copy-start | bytes 7962628
  6.5 36.6 %collective-permute-start.2 = (bf16[528,1152]{1,0:T(8,128)(2,1)}, bf16[528,1152]{1,0:T(8,128)(2,1)}, u32[]{:S(2)}, u32[]{:S(2)}) collective-permute-start(bf16[528,1152]{1,0:T(8,128)(2,1)} %get-tuple-element.42.y0), channel_id=1, source_target_pairs={{0,4},{4,8},{8,12},{12,16},{16,20},{20,24},{24,28},{28,32},{32,36}... | collective-permute-start | bytes 3649544 | tf_op jit(solution)/shard_map/ppermute | solution.py:22
  9.0 34.1 %collective-permute-start = (bf16[528,1152]{1,0:T(8,128)(2,1)}, bf16[528,1152]{1,0:T(8,128)(2,1)}, u32[]{:S(2)}, u32[]{:S(2)}) collective-permute-start(bf16[528,1152]{1,0:T(8,128)(2,1)} %get-tuple-element.41.a0), channel_id=1, source_target_pairs={{0,252},{4,0},{8,4},{12,8},{16,12},{20,16},{24,20},{28,24},{32,28}... | collective-permute-start | bytes 3649544 | tf_op jit(solution)/shard_map/ppermute | solution.py:22
  27.6 1.4 copy-start.6
  30.0 1.4 copy-start.38
  31.4 1.4 copy-start.40
  43.1 31.6 %collective-permute-start.4 = (bf16[528,1152]{1,0:T(8,128)(2,1)}, bf16[528,1152]{1,0:T(8,128)(2,1)}, u32[]{:S(2)}, u32[]{:S(2)}) collective-permute-start(bf16[528,1152]{1,0:T(8,128)(2,1)} %collective-permute-done.2.y1), channel_id=1, source_target_pairs={{0,4},{4,8},{8,12},{12,16},{16,20},{20,24},{24,28},{28,32},{32,36}... | collective-permute-start | bytes 3649544 | tf_op jit(solution)/shard_map/ppermute | solution.py:22
  43.1 31.6 %collective-permute-start.1 = (bf16[528,1152]{1,0:T(8,128)(2,1)}, bf16[528,1152]{1,0:T(8,128)(2,1)}, u32[]{:S(2)}, u32[]{:S(2)}) collective-permute-start(bf16[528,1152]{1,0:T(8,128)(2,1)} %collective-permute-done.a1), channel_id=1, source_target_pairs={{0,252},{4,0},{8,4},{12,8},{16,12},{20,16},{24,20},{28,24},{32,28}... | collective-permute-start | bytes 3649544 | tf_op jit(solution)/shard_map/ppermute | solution.py:22
  50.1 1.7 copy-start.39
  51.7 1.7 copy-start.41
  63.3 1.4 copy-start.30
  64.7 1.4 copy-start.34
  66.1 1.5 copy-start.36
  74.7 62.6 %collective-permute-start.6 = (bf16[528,1152]{1,0:T(8,128)(2,1)}, bf16[528,1152]{1,0:T(8,128)(2,1)}, u32[]{:S(2)}, u32[]{:S(2)}) collective-permute-start(bf16[528,1152]{1,0:T(8,128)(2,1)} %collective-permute-done.4.y2), channel_id=1, source_target_pairs={{0,4},{4,8},{8,12},{12,16},{16,20},{20,24},{24,28},{28,32},{32,36}... | collective-permute-start | bytes 3649544 | tf_op jit(solution)/shard_map/ppermute | solution.py:22
  74.7 62.7 %collective-permute-start.3 = (bf16[528,1152]{1,0:T(8,128)(2,1)}, bf16[528,1152]{1,0:T(8,128)(2,1)}, u32[]{:S(2)}, u32[]{:S(2)}) collective-permute-start(bf16[528,1152]{1,0:T(8,128)(2,1)} %collective-permute-done.1.a2), channel_id=1, source_target_pairs={{0,252},{4,0},{8,4},{12,8},{16,12},{20,16},{24,20},{28,24},{32,28}... | collective-permute-start | bytes 3649544 | tf_op jit(solution)/shard_map/ppermute | solution.py:22
  82.8 1.3 copy-start.3
  84.1 1.7 copy-start.7
  85.8 1.7 copy-start.35
  87.4 1.7 copy-start.37
  89.1 1.3 copy-start.43
  93.2 13.2 %copy-start.11 = (bf16[1152,512]{1,0:T(8,128)(2,1)S(1)}, bf16[1152,512]{1,0:T(8,128)(2,1)}, u32[]{:S(2)}) copy-start(bf16[1152,512]{1,0:T(8,128)(2,1)} %copy-done.10) | copy-start | bytes 3538948
  93.2 13.2 %copy-start.14 = (bf16[1152,512]{1,0:T(8,128)(2,1)S(1)}, bf16[1152,512]{1,0:T(8,128)(2,1)}, u32[]{:S(2)}) copy-start(bf16[1152,512]{1,0:T(8,128)(2,1)} %copy-done.13) | copy-start | bytes 3538948
  105.0 1.4 copy-start.53
  106.4 4.4 %copy-start.16 = (bf16[1152,512]{1,0:T(8,128)(2,1)}, bf16[1152,512]{1,0:T(8,128)(2,1)S(1)}, u32[]{:S(2)}) copy-start(bf16[1152,512]{1,0:T(8,128)(2,1)S(1)} %get-tuple-element.57.a2) | copy-start | bytes 3538948
  106.4 4.4 %copy-start.18 = (bf16[512,1152]{1,0:T(8,128)(2,1)}, bf16[512,1152]{1,0:T(8,128)(2,1)S(1)}, u32[]{:S(2)}) copy-start(bf16[512,1152]{1,0:T(8,128)(2,1)S(1)} %get-tuple-element.58.u0) | copy-start | bytes 3538948
  106.4 4.4 %copy-start.20 = (bf16[512,1152]{1,0:T(8,128)(2,1)}, bf16[512,1152]{1,0:T(8,128)(2,1)S(1)}, u32[]{:S(2)}) copy-start(bf16[512,1152]{1,0:T(8,128)(2,1)S(1)} %get-tuple-element.59.u1) | copy-start | bytes 3538948
  106.4 4.4 %copy-start.22 = (bf16[512,1152]{1,0:T(8,128)(2,1)}, bf16[512,1152]{1,0:T(8,128)(2,1)S(1)}, u32[]{:S(2)}) copy-start(bf16[512,1152]{1,0:T(8,128)(2,1)S(1)} %get-tuple-element.60.u2) | copy-start | bytes 3538948
  106.4 4.4 %copy-start.44 = (bf16[512,1152]{1,0:T(8,128)(2,1)}, bf16[512,1152]{1,0:T(8,128)(2,1)S(1)}, u32[]{:S(2)}) copy-start(bf16[512,1152]{1,0:T(8,128)(2,1)S(1)} %get-tuple-element.68.x2) | copy-start | bytes 3538948
  110.9 19.1 %collective-permute-start.8 = (bf16[576,640]{1,0:T(8,128)(2,1)}, bf16[576,640]{1,0:T(8,128)(2,1)}, u32[]{:S(2)}, u32[]{:S(2)}) collective-permute-start(bf16[576,640]{1,0:T(8,128)(2,1)} %get-tuple-element.61), channel_id=1, source_target_pairs={{0,1},{1,0},{2,3},{3,2},{4,5},{5,4},{6,7},{7,6},{8,9},{9,8},{10,11... | collective-permute-start | bytes 2211848 | tf_op jit(solution)/shard_map/ppermute | solution.py:282
  113.6 16.3 %collective-permute-start.9 = (bf16[576,640]{1,0:T(8,128)(2,1)}, bf16[576,640]{1,0:T(8,128)(2,1)}, u32[]{:S(2)}, u32[]{:S(2)}) collective-permute-start(bf16[576,640]{1,0:T(8,128)(2,1)} %get-tuple-element.62), channel_id=1, source_target_pairs={{0,1},{1,0},{2,3},{3,2},{4,5},{5,4},{6,7},{7,6},{8,9},{9,8},{10,11... | collective-permute-start | bytes 2211848 | tf_op jit(solution)/shard_map/ppermute | solution.py:282
  116.3 1.3 copy-start.17
  120.1 1.3 copy-start.23
  121.4 3.4 %copy-start.31 = (f32[512,1152]{1,0:T(8,128)S(1)}, f32[512,1152]{1,0:T(8,128)}, u32[]{:S(2)}) copy-start(f32[512,1152]{1,0:T(8,128)} %copy-done.30) | copy-start | bytes 7077892
  121.4 3.4 %copy-start.45 = (bf16[512,1152]{1,0:T(8,128)(2,1)S(1)}, bf16[512,1152]{1,0:T(8,128)(2,1)}, u32[]{:S(2)}) copy-start(bf16[512,1152]{1,0:T(8,128)(2,1)} %copy-done.44) | copy-start | bytes 3538948
  128.5 1.4 copy-start.32
  132.9 53.7 %all-to-all-start = ((bf16[16,144,384]{2,1,0:T(8,128)(2,1)}), bf16[16,144,384]{2,1,0:T(8,128)(2,1)}, u32[]{:S(2)}, u32[]{:S(2)}) async-start(bf16[16,144,384]{2,1,0:T(8,128)(2,1)} %copy-done.9), calls=%async_computation | async-start | bytes 3538944 | tf_op jit(solution)/shard_map/all_to_all | solution.py:289
  137.3 76.5 %collective-permute-start.7 = (bf16[528,1152]{1,0:T(8,128)(2,1)}, bf16[528,1152]{1,0:T(8,128)(2,1)}, u32[]{:S(2)}, u32[]{:S(2)}) collective-permute-start(bf16[528,1152]{1,0:T(8,128)(2,1)} %collective-permute-done.6.y3), channel_id=1, source_target_pairs={{0,4},{4,8},{8,12},{12,16},{16,20},{20,24},{24,28},{28,32},{32,36}... | collective-permute-start | bytes 3649544 | tf_op jit(solution)/shard_map/ppermute | solution.py:22
  137.4 76.4 %collective-permute-start.5 = (bf16[528,1152]{1,0:T(8,128)(2,1)}, bf16[528,1152]{1,0:T(8,128)(2,1)}, u32[]{:S(2)}, u32[]{:S(2)}) collective-permute-start(bf16[528,1152]{1,0:T(8,128)(2,1)} %collective-permute-done.3.a3), channel_id=1, source_target_pairs={{0,252},{4,0},{8,4},{12,8},{16,12},{20,16},{24,20},{28,24},{32,28}... | collective-permute-start | bytes 3649544 | tf_op jit(solution)/shard_map/ppermute | solution.py:22
  143.1 1.3 copy-start.4
  144.4 1.7 copy-start.33
  146.0 1.7 copy-start.54
  155.7 1.4 copy-start.26
  157.1 1.4 copy-start.28
  213.8 1.3 copy-start.5
  215.1 1.7 copy-start.8
  218.0 1.7 copy-start.27
  219.7 1.7 copy-start.29
  (18 other events, 19.2 us)
